TPU v7x, 256 devices: a whole 4x4x8 slice. The times are simulated.
256 devices in a mesh: own: 16 (over z, core), pair: 16 (over y, x).
Axes of the slice: x: 4, y: 4, z: 8, core: 2. Of those that a mesh axis runs over, the one named last changes fastest.
Arguments:
- residual: bfloat16 [262144, 512], P(('own', 'pair')), may hold values from -8 to 8
- code_one: int32 [262144], P(('own', 'pair')), may hold values from 0 to 8191, as said below
- code_two: int32 [262144], P(('own', 'pair')), may hold values from 0 to 8191, as said below
Outputs:
- final_residual: bfloat16 [262144, 512], P(('own', 'pair'))
- nearness: bfloat16 [262144, 512], P(('own', 'pair'))
Inputs may be any that keep to these rules, and one draw needn't show every extreme that they name: `code_one`: the owner group of a code is code // 512. Of the 1024 items of one device (devices counted in mesh order, own first), the number whose code lies in owner group o depends only on (o + device) mod 16, is at most 128, and equals 128 for some group on every device. Every code is held by exactly 32 items. `code_two`: same law as code_one, drawn independently.
All inputs are finite; a program needn't handle non-finite values.
Results may differ from a plain program's by a relative error of at most 0.012.
Values may be sent and summed in bfloat16 or wider, within the bound.
A program may use at most 64 MiB of HBM per device.

v0:
```python
import jax
import jax.numpy as jnp
from jax import lax
from jax.sharding import PartitionSpec as P

K = 8192


def route(row_block, codes):
    owner_count = lax.axis_size("own")
    per_owner = K // owner_count
    capacity = 2 * row_block.shape[0] // owner_count
    slot_total = owner_count * capacity
    owner_ids = codes // per_owner
    matches = (owner_ids[:, None] == jnp.arange(owner_count, dtype=jnp.int32)[None, :]).astype(
        jnp.int32
    )
    position = jnp.sum(jnp.cumsum(matches, axis=0) * matches, axis=1) - 1
    target = owner_ids * capacity + position
    source_row = (
        jnp.zeros((slot_total,), jnp.int32)
        .at[target]
        .set(jnp.arange(row_block.shape[0], dtype=jnp.int32))
    )
    live_slot = jnp.zeros((slot_total,), jnp.bool_).at[target].set(True)
    packed = jnp.where(live_slot[:, None], row_block[source_row], jnp.zeros((), row_block.dtype))
    packed_codes = jnp.where(live_slot, codes[source_row], -1)
    got_rows, got_codes = (
        lax.all_to_all(
            packed.reshape(owner_count, capacity, -1),
            "own",
            split_axis=0,
            concat_axis=0,
            tiled=True,
        ),
        lax.all_to_all(
            packed_codes.reshape(owner_count, capacity),
            "own",
            split_axis=0,
            concat_axis=0,
            tiled=True,
        ),
    )
    return (got_rows.reshape(slot_total, -1), got_codes.reshape(slot_total), target)


def centroids(got_rows, got_codes):
    per_owner = K // lax.axis_size("own")
    local_code = got_codes - lax.axis_index("own") * per_owner
    one_hot = (local_code[:, None] == jnp.arange(per_owner, dtype=jnp.int32)[None, :]).astype(
        jnp.bfloat16
    )
    part_sums = lax.dot_general(
        one_hot, got_rows, (((0,), (0,)), ((), ())), preferred_element_type=jnp.float32
    )
    part_counts = jnp.sum(one_hot, axis=0, dtype=jnp.float32)
    code_sums, counts = lax.psum((part_sums, part_counts), "pair")
    centroid = (code_sums / counts[:, None]).astype(jnp.bfloat16)
    picked = centroid[jnp.clip(local_code, 0, per_owner - 1)]
    updated = (got_rows.astype(jnp.float32) - picked.astype(jnp.float32)).astype(jnp.bfloat16)
    return (updated, centroid)


def per_device(residual, code_one, code_two):
    owner_count = lax.axis_size("own")
    capacity = 2 * residual.shape[0] // owner_count
    slot_total = owner_count * capacity
    got_rows, got_codes, target = route(residual, code_one)
    updated, centroid = centroids(got_rows, got_codes)
    returned = lax.all_to_all(
        updated.reshape(owner_count, capacity, -1), "own", split_axis=0, concat_axis=0, tiled=True
    )
    second = returned.reshape(slot_total, -1)[target]
    got_rows, got_codes, target = route(second, code_two)
    updated, centroid = centroids(got_rows, got_codes)
    squares = jnp.sum(jnp.square(got_rows.astype(jnp.float32)), axis=1)
    products = lax.dot_general(
        got_rows, centroid, (((1,), (1,)), ((), ())), preferred_element_type=jnp.float32
    )
    center_sq = jnp.sum(jnp.square(centroid.astype(jnp.float32)), axis=1)
    nearness = (
        (squares[:, None] - 2.0 * products + center_sq[None, :]) / got_rows.shape[1]
    ).astype(jnp.bfloat16)
    final_rows, near_rows = (
        lax.all_to_all(
            updated.reshape(owner_count, capacity, -1),
            "own",
            split_axis=0,
            concat_axis=0,
            tiled=True,
        ),
        lax.all_to_all(
            nearness.reshape(owner_count, capacity, -1),
            "own",
            split_axis=0,
            concat_axis=0,
            tiled=True,
        ),
    )
    return (final_rows.reshape(slot_total, -1)[target], near_rows.reshape(slot_total, -1)[target])


def solution(mesh):
    in_specs = (P(("own", "pair"), None), P(("own", "pair")), P(("own", "pair")))
    out_specs = (P(("own", "pair"), None), P(("own", "pair"), None))
    return jax.shard_map(
        per_device, mesh=mesh, in_specs=in_specs, out_specs=out_specs, check_vma=False
    )
```

profile of v0, /device:TPU:1, one launch (start us, length us, event | category | flops | bytes accessed | tf_op | source)
XLA Modules:
  0.0 615.7 jit_solution(11469807278176427942)
XLA Ops:
  7.2 0.0 copy-start
  7.2 0.0 copy-start.1
  7.2 0.8 add_select_fusion.1
  8.0 4.5 reduce-window.14
  12.5 0.1 slice.34
  12.6 0.1 copy.13
  12.8 0.1 copy.14
  12.8 0.1 broadcast_add_fusion.1
  13.0 0.7 broadcast_clamp_fusion.2
  13.7 4.3 scatter_custom_fusion.3
  18.0 0.0 copy-done.1
  18.0 0.0 copy-start.2
  18.0 8.6 %gather_fusion.5 = s32[2048]{0:T(1024)S(1)} fusion(s32[1024]{0:T(1024)S(1)} %copy-done.1, s32[2048]{0:T(1024)S(1)} %fusion.16), kind=kCustom, calls=%fused_computation.5 | custom fusion | bytes 24576 | tf_op jit(solution)/shard_map/gather | solution.py:27
  26.6 4.3 scatter_custom_fusion
  31.0 0.6 broadcast_select_fusion.2
  31.6 10.0 %all-to-all-start.4 = ((s32[16,1,128]{2,1,0:T(1,128)}), s32[16,1,128]{2,1,0:T(1,128)S(1)}, u32[]{:S(2)}, u32[]{:S(2)}) async-start(s32[16,1,128]{2,1,0:T(1,128)} %bitcast.17), calls=%async_computation.4 | async-start | bytes 16384 | tf_op jit(solution)/shard_map/all_to_all | solution.py:36
  41.6 0.0 copy-done.2
  41.6 4.5 reduce-window.16
  46.1 0.1 slice.36
  46.2 0.1 copy.15
  46.4 0.1 copy.16
  46.4 0.1 broadcast_add_fusion
  46.6 4.3 scatter_custom_fusion.1
  50.9 4.5 scatter_custom_fusion.2
  55.5 8.6 %gather_fusion.1 = s32[2048]{0:T(1024)S(1)} fusion(s32[1024]{0:T(1024)S(1)} %copy-done.2, s32[2048]{0:T(1024)S(1)} %fusion.15), kind=kCustom, calls=%fused_computation.1 | custom fusion | bytes 24576 | tf_op jit(solution)/shard_map/gather | solution.py:27
  64.1 0.6 broadcast_select_fusion.3
  64.7 7.5 %gather_fusion = bf16[2048,512]{1,0:T(8,128)(2,1)S(1)} fusion(bf16[1024,512]{1,0:T(8,128)(2,1)S(1)} %copy-done, s32[2048]{0:T(1024)S(1)} %fusion.15), kind=kCustom, calls=%fused_computation | custom fusion | bytes 4202496 | tf_op jit(solution)/shard_map/gather | solution.py:26
  72.2 0.0 all-to-all-done.4
  72.2 7.2 %all-to-all-start.1 = ((s32[16,1,128]{2,1,0:T(1,128)}), s32[16,1,128]{2,1,0:T(1,128)S(1)}, u32[]{:S(2)}, u32[]{:S(2)}) async-start(s32[16,1,128]{2,1,0:T(1,128)} %bitcast.9), calls=%async_computation.1 | async-start | bytes 16384 | tf_op jit(solution)/shard_map/all_to_all | solution.py:36
  79.5 1.6 broadcast_select_fusion
  81.0 5.4 all-to-all-done.1
  86.4 4.2 all-to-all-start
  90.6 0.0 all-reduce.4.cloned.1.call-start
  90.7 48.9 %all-to-all-done = bf16[16,128,512]{2,1,0:T(8,128)(2,1)S(1)} async-done(((bf16[16,128,512]{2,1,0:T(8,128)(2,1)}), bf16[16,128,512]{2,1,0:T(8,128)(2,1)S(1)}, u32[]{:S(2)}, u32[]{:S(2)}) %all-to-all-start) | async-done | bytes 2097184 | tf_op jit(solution)/shard_map/all_to_all | solution.py:29
  139.5 2.6 fusion.6
  142.2 0.0 copy-done.3
  142.2 0.0 all-reduce.4.cloned.1.call-update
  142.2 0.0 all-reduce.6.cloned.1.call-start
  142.2 0.6 convert_reduce_fusion.1
  142.8 0.6 convert_reduce_fusion
  143.4 33.8 %all-reduce = (f32[512]{0:T(512)S(1)}, f32[512]{0:T(512)S(1)}) all-reduce(f32[512]{0:T(512)S(1)} %convert_reduce_fusion.1, f32[512]{0:T(512)S(1)} %convert_reduce_fusion), channel_id=1, replica_groups=mesh['own'=16,'pair'=16] {'pair'}, use_global_device_ids=true, to_apply=%region_11.12 | all-reduce | flops 1024 | bytes 8192 | tf_op jit(solution)/shard_map/psum | solution.py:57
  177.2 59.6 %all-reduce.4.cloned.1.call-done = f32[512,512]{1,0:T(8,128)} async-done(((f32[512,512]{1,0:T(8,128)}), f32[512,512]{1,0:T(8,128)}) %all-reduce.4.cloned.1.call-update) | async-done | bytes 1048592 | tf_op jit(solution)/shard_map/psum | solution.py:57
  236.8 1.4 divide_convert_fusion.1
  238.2 9.2 %gather_fusion.2 = bf16[2048,512]{1,0:T(8,128)(2,1)} fusion(bf16[512,512]{1,0:T(8,128)(2,1)S(1)} %divide_convert_fusion.1, s32[2048]{0:T(1024)S(1)} %broadcast_clamp_fusion.1), kind=kCustom, calls=%fused_computation.2 | custom fusion | bytes 4202496 | tf_op jit(solution)/shard_map/gather | solution.py:59
  247.4 2.9 fusion.2
  250.3 60.1 %all_to_all.43 = bf16[16,128,512]{2,1,0:T(8,128)(2,1)} all-to-all(bf16[16,128,512]{2,1,0:T(8,128)(2,1)S(1)} %fusion.2), channel_id=1, replica_groups=mesh['own'=16,'pair'=16] {'own'}, dimensions={0} | all-to-all | bytes 4194304 | tf_op jit(solution)/shard_map/all_to_all | solution.py:70
  310.4 5.8 gather_fusion.3
  316.3 9.2 %gather_fusion.4 = bf16[2048,512]{1,0:T(8,128)(2,1)} fusion(bf16[1024,512]{1,0:T(8,128)(2,1)S(1)} %gather_fusion.3, s32[2048]{0:T(1024)S(1)} %fusion.16), kind=kCustom, calls=%fused_computation.4 | custom fusion | bytes 4202496 | tf_op jit(solution)/shard_map/gather | solution.py:26
  325.5 1.8 broadcast_select_fusion.1
  327.2 53.7 %all_to_all.44 = bf16[16,128,512]{2,1,0:T(8,128)(2,1)S(1)} all-to-all(bf16[16,128,512]{2,1,0:T(8,128)(2,1)S(1)} %broadcast_select_fusion.1), channel_id=1, replica_groups=mesh['own'=16,'pair'=16] {'own'}, dimensions={0} | all-to-all | bytes 4194304 | tf_op jit(solution)/shard_map/all_to_all | solution.py:29
  381.0 1.3 copy-done.4
  382.3 2.6 fusion.4
  384.9 0.0 all-reduce.6.cloned.1.call-update
  385.0 90.3 %all-reduce.6.cloned.1.call-done = f32[512,512]{1,0:T(8,128)} async-done(((f32[512,512]{1,0:T(8,128)}), f32[512,512]{1,0:T(8,128)}) %all-reduce.6.cloned.1.call-update) | async-done | bytes 1048592 | tf_op jit(solution)/shard_map/psum | solution.py:57
  475.3 1.5 multiply_reduce_fusion
  476.8 9.2 %gather_fusion.6 = bf16[2048,512]{1,0:T(8,128)(2,1)} fusion(bf16[512,512]{1,0:T(8,128)(2,1)S(1)} %get-tuple-element.5, s32[2048]{0:T(1024)S(1)} %broadcast_clamp_fusion), kind=kCustom, calls=%fused_computation.6 | custom fusion | bytes 4202496 | tf_op jit(solution)/shard_map/gather | solution.py:59
  486.0 4.4 fusion.1
  490.4 0.0 copy-done.5
  490.4 1.4 multiply_convert_fusion
  491.8 60.1 %all_to_all.45 = bf16[16,128,512]{2,1,0:T(8,128)(2,1)} all-to-all(bf16[16,128,512]{2,1,0:T(8,128)(2,1)S(1)} %bitcast.75), channel_id=1, replica_groups=mesh['own'=16,'pair'=16] {'own'}, dimensions={0} | all-to-all | bytes 4194304 | tf_op jit(solution)/shard_map/all_to_all | solution.py:92
  551.9 3.6 all-to-all-start.5
  555.6 7.0 %gather_fusion.8 = bf16[1024,512]{1,0:T(8,128)(2,1)} fusion(bf16[2048,512]{1,0:T(8,128)(2,1)} %bitcast.67, s32[1024]{0:T(1024)S(1)} %get-tuple-element.6), kind=kCustom, calls=%fused_computation.8 | custom fusion | bytes 2101248 | tf_op jit(solution)/shard_map/gather | solution.py:100
  562.5 41.3 %all-to-all-done.5 = bf16[16,128,512]{2,1,0:T(8,128)(2,1)S(1)} async-done(((bf16[16,128,512]{2,1,0:T(8,128)(2,1)}), bf16[16,128,512]{2,1,0:T(8,128)(2,1)S(1)}, u32[]{:S(2)}, u32[]{:S(2)}) %all-to-all-start.5) | async-done | bytes 2097184 | tf_op jit(solution)/shard_map/all_to_all | solution.py:85
  603.8 5.1 gather_fusion.7
  (22 shorter events, 0.2 us)
Async XLA Ops:
  7.2 57.5 %copy-start = (bf16[1024,512]{1,0:T(8,128)(2,1)S(1)}, bf16[1024,512]{1,0:T(8,128)(2,1)}, u32[]{:S(2)}) copy-start(bf16[1024,512]{1,0:T(8,128)(2,1)} %param.3) | copy-start | bytes 3145732
  7.2 10.8 %copy-start.1 = (s32[1024]{0:T(1024)S(1)}, s32[1024]{0:T(1024)}, u32[]{:S(2)}) copy-start(s32[1024]{0:T(1024)} %param.5) | copy-start | bytes 12292
  18.0 23.6 %copy-start.2 = (s32[1024]{0:T(1024)S(1)}, s32[1024]{0:T(1024)}, u32[]{:S(2)}) copy-start(s32[1024]{0:T(1024)} %param.4) | copy-start | bytes 12292
  31.6 40.6 %all-to-all-start.4 = ((s32[16,1,128]{2,1,0:T(1,128)}), s32[16,1,128]{2,1,0:T(1,128)S(1)}, u32[]{:S(2)}, u32[]{:S(2)}) async-start(s32[16,1,128]{2,1,0:T(1,128)} %bitcast.17), calls=%async_computation.4 | async-start | bytes 16384 | tf_op jit(solution)/shard_map/all_to_all | solution.py:36
  72.2 14.2 %all-to-all-start.1 = ((s32[16,1,128]{2,1,0:T(1,128)}), s32[16,1,128]{2,1,0:T(1,128)S(1)}, u32[]{:S(2)}, u32[]{:S(2)}) async-start(s32[16,1,128]{2,1,0:T(1,128)} %bitcast.9), calls=%async_computation.1 | async-start | bytes 16384 | tf_op jit(solution)/shard_map/all_to_all | solution.py:36
  86.4 53.1 %all-to-all-start = ((bf16[16,128,512]{2,1,0:T(8,128)(2,1)}), bf16[16,128,512]{2,1,0:T(8,128)(2,1)S(1)}, u32[]{:S(2)}, u32[]{:S(2)}) async-start(bf16[16,128,512]{2,1,0:T(8,128)(2,1)} %broadcast_select_fusion), calls=%async_computation | async-start | bytes 4194304 | tf_op jit(solution)/shard_map/all_to_all | solution.py:29
  90.6 146.3 %all-reduce.4.cloned.1.call-start = ((), (), s32[]{:S(2)}) async-start(), calls=%async_computation.7 | async-start | bytes 2097152 | tf_op jit(solution)/shard_map/psum | solution.py:57
  139.5 2.6 copy-start.3
  142.2 333.1 %all-reduce.6.cloned.1.call-start = ((), (), s32[]{:S(2)}) async-start(), calls=%async_computation.8 | async-start | bytes 2097152 | tf_op jit(solution)/shard_map/psum | solution.py:57
  381.0 1.4 copy-start.4
  486.0 4.4 copy-start.5
  551.9 51.9 %all-to-all-start.5 = ((bf16[16,128,512]{2,1,0:T(8,128)(2,1)}), bf16[16,128,512]{2,1,0:T(8,128)(2,1)S(1)}, u32[]{:S(2)}, u32[]{:S(2)}) async-start(bf16[16,128,512]{2,1,0:T(8,128)(2,1)} %get-tuple-element.15), calls=%async_computation.5 | async-start | bytes 4194304 | tf_op jit(solution)/shard_map/all_to_all | solution.py:85
Sparse Core Ops, SparseCore 0:
  142.3 94.4 all-reduce.3
  385.1 90.1 all-reduce.5
where the time goes:
time: 616 us
  waiting for transfers between devices  245 us (40%)
  blocking collectives  208 us (34%)
  local copies, waits for them, and re-layouts  89.6 us (15%)
  other arithmetic  26.8 us (4%)
  starting transfers between devices  25.1 us (4%)
  between operations  14.3 us (2%)
  matrix products  6.68 us (1%)
    psum x2, waiting for transfers between devices, centroids(): code_sums, counts = lax.psum((part_sums, part_counts), 'pair')  150 us
    all_to_all x1, blocking collectives, per_device(): lax.all_to_all(nearness.reshape(owner_count, capacity, -1), 'own', split_...  60.1 us
    all_to_all x1, blocking collectives, per_device(): lax.all_to_all(updated.reshape(owner_count, capacity, -1), 'own', split_a...  60.1 us
    all_to_all x1, blocking collectives, route(): lax.all_to_all(packed.reshape(owner_count, capacity, -1), 'own', split_ax...  53.7 us
    all_to_all x1, waiting for transfers between devices, route(): lax.all_to_all(packed.reshape(owner_count, capacity, -1), 'own', split_ax...  48.9 us
    all_to_all x1, waiting for transfers between devices, per_device(): lax.all_to_all(updated.reshape(owner_count, capacity, -1), 'own', split_a...  41.3 us
    psum x1, blocking collectives, centroids(): code_sums, counts = lax.psum((part_sums, part_counts), 'pair')  33.8 us
    gather x2, local copies, waits for them, and re-layouts, centroids(): picked = centroid[jnp.clip(local_code, 0, per_owner - 1)]  18.3 us
  transfers between devices with their start and end apart: 6, of which 5 were waited for; matrix products, arithmetic and copies ran while one was open for 7% of the time, Pallas kernels for 0%

commit v1 on v0

v1 whole, which is shorter than its diff:
```python
import functools

import jax
import jax.numpy as jnp
from jax import lax
from jax.experimental import pallas as pl
from jax.experimental.pallas import tpu as pltpu
from jax.sharding import PartitionSpec as P

ROWS = 1024
D = 512
GROUPS = 16
CAP = 128
SLOTS = GROUPS * CAP
GCODES = 512
ITEMS_PER_CODE = 32
CHUNKS = 2
W = D // CHUNKS
HALF = GCODES // 2
ZN = 8
ZC = HALF // ZN
BF = jnp.bfloat16
F32 = jnp.float32
I32 = jnp.int32
NT = (((1,), (1,)), ((), ()))


def iota(shape, dim):
    return lax.broadcasted_iota(I32, shape, dim)


def hot(mask):
    return jnp.where(mask, 1.0, 0.0).astype(BF)


def prep_kernel(lane_ref, col_ref, rows_ref, packed_ref, send_ref, scol_ref, item_ref, tgt_ref):
    codes = lane_ref[...]
    groups = lax.shift_right_logical(codes, 9)
    member = jnp.concatenate(
        [
            iota((GROUPS, ROWS), 0) == groups[0:1, :],
            iota((GROUPS, ROWS), 0) == groups[1:2, :],
        ],
        axis=0,
    )
    before = hot(iota((ROWS, ROWS), 0) < iota((ROWS, ROWS), 1))
    rank = jnp.dot(hot(member), before, preferred_element_type=F32)
    rank = jnp.where(member, rank, 0.0)
    target = []
    for level in range(2):
        r = jnp.sum(rank[level * GROUPS : (level + 1) * GROUPS], axis=0, keepdims=True)
        target.append(groups[level : level + 1] * CAP + r.astype(I32))
    gcol = lax.shift_right_logical(col_ref[...], 9)[:, 1:2]
    mcol = iota((ROWS, 128), 1) == gcol
    after = hot(iota((ROWS, ROWS), 0) > iota((ROWS, ROWS), 1))
    rcol = jnp.dot(after, hot(mcol), preferred_element_type=F32)
    rcol = jnp.sum(jnp.where(mcol, rcol, 0.0), axis=1, keepdims=True)
    tgt_ref[...] = gcol * CAP + rcol.astype(I32)

    item = iota((1, ROWS), 1)
    send_ref[...] = jnp.zeros_like(send_ref)
    for level in range(2):
        local = jnp.bitwise_and(codes[level : level + 1], GCODES - 1)
        feats = jnp.concatenate(
            [
                lax.shift_right_logical(local, 4),
                jnp.bitwise_and(local, 15),
                lax.shift_right_logical(item, 5),
                jnp.bitwise_and(item, 31),
                jnp.ones_like(item),
                jnp.zeros((3, ROWS), I32),
            ],
            axis=0,
        ).astype(F32).astype(BF)

        def block(o, carry, level=level, feats=feats):
            base = pl.multiple_of(o * CAP, CAP)
            place = hot(iota((CAP, ROWS), 0) + base == target[level])
            if level == 0:
                got = jnp.dot(place, rows_ref[...], preferred_element_type=F32).astype(BF)
                for ch in range(CHUNKS):
                    packed_ref[ch, o] = got[:, ch * W : (ch + 1) * W]
            lanes = lax.dot_general(feats, place, NT, preferred_element_type=F32)
            live = lanes[4:5]
            send_ref[o, level : level + 1, :] = (lanes[0:1] * 16.0 + lanes[1:2] + live - 1.0).astype(I32)
            if level == 0:
                item_ref[o] = jnp.broadcast_to(lanes[2:3] * 32.0 + lanes[3:4] + live - 1.0, (8, CAP)).astype(I32)
            cols = lax.dot_general(place, feats, NT, preferred_element_type=F32)
            alive = cols[:, 4:5]
            code = (cols[:, 0:1] * 16.0 + cols[:, 1:2] + alive - 1.0).astype(I32)
            scol_ref[level, o, :, 0:1] = code
            which = (cols[:, 2:3] * 32.0 + cols[:, 3:4] + 2.0 * alive - 2.0).astype(I32)
            scol_ref[level, o, :, 1:2] = which
            return carry

        lax.fori_loop(0, GROUPS, block, 0)


def main_kernel(
    packed1, send_codes, scol, item1, tgt2,
    final_out, near_out,
    got_codes, packed2, got, acc, half_out, half_in, zpart, zin, table, move, back, secp, finp, nearacc, nearp,
    code_s, code_r, a2a_s, a2a_r, hs, hr, rzs, rzr, azs, azr, xs, xr, ss, sr,
):
    own = lax.axis_index("own")
    me = lax.axis_index("pair")
    z, c = lax.div(own, 2), lax.rem(own, 2)
    y, x = lax.div(me, 4), lax.rem(me, 4)
    sib = z * 2 + (1 - c)

    def at(dy, dx):
        return lax.rem(y + dy, 4) * 4 + lax.rem(x + dx, 4)

    def zat(dz):
        return lax.rem(z + dz, ZN) * 2 + c

    barrier = pltpu.get_barrier_semaphore()

    def greet(o, p):
        pl.semaphore_signal(barrier, inc=1, device_id=(o, p), device_id_type=pl.DeviceIdType.MESH)

    for d in range(1, 16):
        greet(own, at(d // 4, d % 4))
    for dz in range(1, ZN):
        greet(zat(dz), me)
    greet(sib, me)
    pl.semaphore_wait(barrier, 15 + ZN - 1 + 1)

    started = []

    def copy(src, dst, s, r, o, p):
        return pltpu.make_async_remote_copy(
            src_ref=src, dst_ref=dst, send_sem=s, recv_sem=r,
            device_id=(o, p), device_id_type=pl.DeviceIdType.MESH,
        )

    def send(src, dst, s, r, o, p):
        k = copy(src, dst, s, r, o, p)
        k.start()
        started.append(k)

    def arrive(dst, s, r):
        copy(dst, dst, s, r, own, at(0, 1)).wait_recv()

    packs = (packed1, packed2)
    order = [(0, 1), (1, 0), (0, 3), (3, 0), (1, 1), (3, 3), (1, 3), (3, 1),
             (0, 2), (2, 0), (1, 2), (2, 1), (3, 2), (2, 3), (2, 2)]

    def send_rows(l, ch, dy, dx):
        d = dy * 4 + dx
        to = at(dy, dx)
        send(packs[l].at[ch, to], got.at[l, ch, d], a2a_s.at[l, ch, d], a2a_r.at[l, ch, d], own, to)

    def sum_rows(l, ch):
        got[l, ch, 0] = packs[l][ch, me]
        for q in range(4):
            for d in range(4 * q, 4 * q + 4):
                if d:
                    arrive(got.at[l, ch, d], a2a_s.at[l, ch, d], a2a_r.at[l, ch, d])
                    if l == 0 and ch == 0:
                        arrive(got_codes.at[d], code_s.at[d], code_r.at[d])
            codes = jnp.concatenate([got_codes[d, l : l + 1, :] for d in range(4 * q, 4 * q + 4)], axis=1)
            pick = hot(iota((GCODES, 4 * CAP), 0) == codes)
            part = jnp.dot(pick, got[l, ch, 4 * q : 4 * q + 4].reshape(4 * CAP, W), preferred_element_type=F32)
            if q == 0:
                acc[ch] = part
            else:
                acc[ch] += part
        half_out[l, ch] = acc[ch, pl.ds(pl.multiple_of((1 - c) * HALF, HALF), HALF)].astype(BF)
        send(half_out.at[l, ch], half_in.at[l, ch], hs.at[l, ch], hr.at[l, ch], sib, me)

    def reduce_z(l, ch):
        arrive(half_in.at[l, ch], hs.at[l, ch], hr.at[l, ch])
        mine = pl.ds(pl.multiple_of(c * HALF, HALF), HALF)
        both = acc[ch, mine] + half_in[l, ch].astype(F32)
        acc[ch, mine] = both
        zpart[l, ch] = both.astype(BF)
        for dz in (1, 7, 2, 6, 3, 5, 4):
            to = lax.rem(z + dz, ZN)
            send(zpart.at[l, ch, pl.ds(pl.multiple_of(to * ZC, ZC), ZC)], zin.at[l, ch, dz],
                 rzs.at[l, ch, dz], rzr.at[l, ch, dz], zat(dz), me)

    def gather_z(l, ch):
        total = acc[ch, pl.ds(pl.multiple_of(c * HALF + z * ZC, ZC), ZC)]
        for dz in range(1, ZN):
            arrive(zin.at[l, ch, dz], rzs.at[l, ch, dz], rzr.at[l, ch, dz])
            total += zin[l, ch, dz].astype(F32)
        mine = pl.ds(pl.multiple_of(z * ZC, ZC), ZC)
        table[l, ch, 0, c, mine, :] = (total * (1.0 / ITEMS_PER_CODE)).astype(BF)
        for dz in (1, 7, 2, 6, 3, 5, 4):
            here = table.at[l, ch, 0, c, mine]
            send(here, here, azs.at[l, ch, dz], azr.at[l, ch, dz], zat(dz), me)

    def slot(ch, da, db):
        return da * 4 + db if ch % 2 == 0 else db * 4 + da

    def side(ch, da, db):
        return at(da, db) if ch % 2 == 0 else at(db, da)

    def to_sibling(l, ch, s):
        here = table.at[l, ch, s, c]
        send(here, here, ss.at[l, ch, s], sr.at[l, ch, s], sib, me)

    def pass_on(l, ch, source, dest, k, da, db, part):
        if part is None:
            a, b = table.at[l, ch, source, c], table.at[l, ch, dest, c]
        else:
            rows = pl.ds(part * (HALF // 2), HALF // 2)
            a, b = table.at[l, ch, source, c, rows], table.at[l, ch, dest, c, rows]
        send(a, b, xs.at[l, ch, k], xr.at[l, ch, k], own, side(ch, da, db))

    def come(l, ch, dest, k, part=None):
        if part is None:
            b = table.at[l, ch, dest, c]
        else:
            b = table.at[l, ch, dest, c, pl.ds(part * (HALF // 2), HALF // 2)]
        arrive(b, xs.at[l, ch, k], xr.at[l, ch, k])

    def second_axis(l, ch, da):
        s = slot(ch, da, 0)
        pass_on(l, ch, s, slot(ch, da, 1), 4 + 4 * da, 0, 1, None)
        pass_on(l, ch, s, slot(ch, da, 3), 5 + 4 * da, 0, 3, None)

    def start_plane(l, ch):
        here = table.at[l, ch, 0, c, pl.ds(0, ZC)]
        for dz in range(1, ZN):
            arrive(here, azs.at[l, ch, dz], azr.at[l, ch, dz])
        pass_on(l, ch, 0, slot(ch, 1, 0), 0, 1, 0, None)
        pass_on(l, ch, 0, slot(ch, 3, 0), 1, 3, 0, None)
        second_axis(l, ch, 0)
        to_sibling(l, ch, 0)

    def first_hop(l, ch, da):
        s, k = slot(ch, da, 0), (0 if da == 1 else 1)
        come(l, ch, s, k)
        if da == 1:
            pass_on(l, ch, s, slot(ch, 2, 0), 2, 1, 0, 0)
        else:
            pass_on(l, ch, s, slot(ch, 2, 0), 3, 3, 0, 1)
        second_axis(l, ch, da)
        to_sibling(l, ch, s)

    def first_far(l, ch):
        s = slot(ch, 2, 0)
        come(l, ch, s, 2, 0)
        come(l, ch, s, 3, 1)
        second_axis(l, ch, 2)
        to_sibling(l, ch, s)

    def second_hop(l, ch, da):
        s = slot(ch, da, 1)
        come(l, ch, s, 4 + 4 * da)
        pass_on(l, ch, s, slot(ch, da, 2), 6 + 4 * da, 0, 1, 0)
        to_sibling(l, ch, s)
        s = slot(ch, da, 3)
        come(l, ch, s, 5 + 4 * da)
        pass_on(l, ch, s, slot(ch, da, 2), 7 + 4 * da, 0, 3, 1)
        to_sibling(l, ch, s)

    def second_far(l, ch, da):
        s = slot(ch, da, 2)
        come(l, ch, s, 6 + 4 * da, 0)
        come(l, ch, s, 7 + 4 * da, 1)
        to_sibling(l, ch, s)

    def plane(l, ch, use):
        first_hop(l, ch, 1)
        first_hop(l, ch, 3)
        second_hop(l, ch, 0)
        use(slot(ch, 0, 0))
        first_far(l, ch)
        second_hop(l, ch, 1)
        second_hop(l, ch, 3)
        use(slot(ch, 1, 0))
        use(slot(ch, 3, 0))
        use(slot(ch, 0, 1))
        use(slot(ch, 0, 3))
        second_hop(l, ch, 2)
        second_far(l, ch, 0)
        second_far(l, ch, 1)
        second_far(l, ch, 3)
        use(slot(ch, 2, 0))
        for da in (1, 3):
            use(slot(ch, da, 1))
            use(slot(ch, da, 3))
        second_far(l, ch, 2)
        for da, db in ((0, 2), (2, 1), (2, 3), (1, 2), (3, 2), (2, 2)):
            use(slot(ch, da, db))

    def ready(l, ch, s):
        arrive(table.at[l, ch, s, 1 - c], ss.at[l, ch, s], sr.at[l, ch, s])
        o = at((4 - s // 4) % 4, (4 - s % 4) % 4)
        pick = hot(iota((CAP, GCODES), 1) == scol[l, o, :, 0:1])
        cents = table[l, ch, s].reshape(GCODES, W)
        return o, cents, jnp.dot(pick, cents, preferred_element_type=F32)

    def use_one(ch, s):
        o, _, picked = ready(0, ch, s)
        rows = (packed1[ch, o].astype(F32) - picked).astype(BF)
        secp[ch, pl.ds(pl.multiple_of(o * CAP, CAP), CAP), :] = rows

    def use_two(ch, s):
        o, cents, picked = ready(1, ch, s)
        place = pl.ds(pl.multiple_of(o * CAP, CAP), CAP)
        rows = packed2[ch, o]
        wide = rows.astype(F32)
        finp[ch, place, :] = (wide - picked).astype(BF)
        prods = lax.dot_general(rows, cents, NT, preferred_element_type=F32)
        sq = jnp.sum(wide * wide, axis=1, keepdims=True)
        cw = cents.astype(F32)
        cw = cw * cw
        top = cw.astype(BF)
        low = (cw - top.astype(F32)).astype(BF)
        ones = jnp.ones((8, W), BF)
        csq = lax.dot_general(ones, top, NT, preferred_element_type=F32)
        csq += lax.dot_general(ones, low, NT, preferred_element_type=F32)
        part = sq - 2.0 * prods + csq[0:1]
        if ch == 0:
            nearacc[place, :] = part
        elif ch < CHUNKS - 1:
            nearacc[place, :] += part
        else:
            nearp[place, :] = ((nearacc[place, :] + part) * (1.0 / D)).astype(BF)

    for dy, dx in order:
        d = dy * 4 + dx
        send(send_codes.at[at(dy, dx)], got_codes.at[d], code_s.at[d], code_r.at[d], own, at(dy, dx))
    got_codes[0] = send_codes[me]
    for ch in range(CHUNKS):
        for dy, dx in order:
            send_rows(0, ch, dy, dx)

    first_items = jnp.concatenate([item1[o, 0:1, :] for o in range(GROUPS)], axis=1)

    def build_move(o, carry):
        move[pl.ds(pl.multiple_of(o * CAP, CAP), CAP), :] = hot(first_items == scol[1, o, :, 1:2])
        return carry

    lax.fori_loop(0, GROUPS, build_move, 0)

    def build_back(b, carry):
        rows = pl.ds(pl.multiple_of(b * CAP, CAP), CAP)
        back[rows, :] = hot(iota((CAP, SLOTS), 1) == tgt2[rows, :])
        return carry

    lax.fori_loop(0, ROWS // CAP, build_back, 0)

    for l in range(2):
        for ch in range(CHUNKS):
            sum_rows(l, ch)
            reduce_z(l, ch)
            gather_z(l, ch)
            start_plane(l, ch)
        for ch in range(CHUNKS):
            if l == 0:
                plane(l, ch, functools.partial(use_one, ch))
                for dy in range(4):
                    oy = lax.rem(y + dy, 4)
                    rows = move[pl.ds(pl.multiple_of(oy * (4 * CAP), 4 * CAP), 4 * CAP), :]
                    moved = jnp.dot(rows, secp[ch], preferred_element_type=F32).astype(BF)
                    packed2[ch, pl.ds(oy * 4, 4)] = moved.reshape(4, CAP, W)
                    for dx in (1, 3, 0, 2):
                        if dy or dx:
                            send_rows(1, ch, dy, dx)
            else:
                plane(l, ch, functools.partial(use_two, ch))
                for b in range(2):
                    rows = back[b * 512 : (b + 1) * 512, :]
                    out = jnp.dot(rows, finp[ch], preferred_element_type=F32).astype(BF)
                    final_out[b * 512 : (b + 1) * 512, ch * W : (ch + 1) * W] = out
    for b in range(2):
        rows = back[b * 512 : (b + 1) * 512, :]
        near_out[b * 512 : (b + 1) * 512, :] = jnp.dot(rows, nearp[...], preferred_element_type=F32).astype(BF)
    for k in started:
        k.wait_send()


def vmem(n):
    return [pl.BlockSpec(memory_space=pltpu.VMEM)] * n


def per_device(residual, code_one, code_two):
    lanes = jnp.stack([code_one, code_two], axis=0)
    cols = jnp.stack([code_one, code_two], axis=1)
    packed, codes, scol, item, tgt = pl.pallas_call(
        prep_kernel,
        out_shape=(
            jax.ShapeDtypeStruct((CHUNKS, GROUPS, CAP, W), BF),
            jax.ShapeDtypeStruct((GROUPS, 8, CAP), I32),
            jax.ShapeDtypeStruct((2, GROUPS, CAP, 2), I32),
            jax.ShapeDtypeStruct((GROUPS, 8, CAP), I32),
            jax.ShapeDtypeStruct((ROWS, 1), I32),
        ),
        in_specs=vmem(3),
        out_specs=tuple(vmem(5)),
        compiler_params=pltpu.CompilerParams(vmem_limit_bytes=50 * 1024 * 1024),
    )(lanes, cols, residual)
    dma = pltpu.SemaphoreType.DMA
    C = CHUNKS
    out = pl.pallas_call(
        main_kernel,
        out_shape=(
            jax.ShapeDtypeStruct((ROWS, D), BF),
            jax.ShapeDtypeStruct((ROWS, D), BF),
        ),
        in_specs=vmem(5),
        out_specs=tuple(vmem(2)),
        scratch_shapes=[
            pltpu.VMEM((GROUPS, 8, CAP), I32),
            pltpu.VMEM((C, GROUPS, CAP, W), BF),
            pltpu.VMEM((2, C, GROUPS, CAP, W), BF),
            pltpu.VMEM((C, GCODES, W), F32),
            pltpu.VMEM((2, C, HALF, W), BF),
            pltpu.VMEM((2, C, HALF, W), BF),
            pltpu.VMEM((2, C, HALF, W), BF),
            pltpu.VMEM((2, C, ZN, ZC, W), BF),
            pltpu.VMEM((2, C, GROUPS, 2, HALF, W), BF),
            pltpu.VMEM((SLOTS, SLOTS), BF),
            pltpu.VMEM((ROWS, SLOTS), BF),
            pltpu.VMEM((C, SLOTS, W), BF),
            pltpu.VMEM((C, SLOTS, W), BF),
            pltpu.VMEM((SLOTS, D), F32),
            pltpu.VMEM((SLOTS, D), BF),
            dma((GROUPS,)), dma((GROUPS,)),
            dma((2, C, GROUPS)), dma((2, C, GROUPS)),
            dma((2, C)), dma((2, C)),
            dma((2, C, ZN)), dma((2, C, ZN)),
            dma((2, C, ZN)), dma((2, C, ZN)),
            dma((2, C, 20)), dma((2, C, 20)),
            dma((2, C, GROUPS)), dma((2, C, GROUPS)),
        ],
        compiler_params=pltpu.CompilerParams(
            collective_id=0, has_side_effects=True, vmem_limit_bytes=60 * 1024 * 1024
        ),
    )(packed, codes, scol, item, tgt)
    return out


def solution(mesh):
    in_specs = (P(("own", "pair"), None), P(("own", "pair")), P(("own", "pair")))
    out_specs = (P(("own", "pair"), None), P(("own", "pair"), None))
    return jax.shard_map(
        per_device, mesh=mesh, in_specs=in_specs, out_specs=out_specs, check_vma=False
    )
```

time: 616 us -> 232 us (0.38)
  waiting for transfers between devices: 245 us -> 0 us
  Pallas kernels: 0 us -> 223 us
  blocking collectives: 208 us -> 0 us
  local copies, waits for them, and re-layouts: 89.6 us -> 6.81 us
  other arithmetic: 26.8 us -> 1.43 us
  starting transfers between devices: 25.1 us -> 0 us
  between operations: 14.3 us -> 0.67 us
  matrix products: 6.68 us -> 0 us
    pallas_call x0 -> x2, Pallas kernels: none -> 223 us  [the longest x1 203 us: per_device(): pl.pallas_call(main_kernel, out_shape=(jax.ShapeDtypeStruct((ROWS, D), BF...]
    all_to_all x3 -> x0, blocking collectives: 174 us -> none  [the longest x1 60.1 us: per_device(): lax.all_to_all(nearness.reshape(owner_count, capacity, -1), 'own', split_...]
    psum x2 -> x0, waiting for transfers between devices: 150 us -> none  [centroids(): code_sums, counts = lax.psum((part_sums, part_counts), 'pair')]
    all_to_all x4 -> x0, waiting for transfers between devices: 95.5 us -> none  [the longest x1 48.9 us: route(): lax.all_to_all(packed.reshape(owner_count, capacity, -1), 'own', split_ax...]
    gather x9 -> x0, local copies, waits for them, and re-layouts: 70.1 us -> none  [the longest x2 18.3 us: centroids(): picked = centroid[jnp.clip(local_code, 0, per_owner - 1)]]
    psum x1 -> x0, blocking collectives: 33.8 us -> none  [centroids(): code_sums, counts = lax.psum((part_sums, part_counts), 'pair')]
    all_to_all x4 -> x0, starting transfers between devices: 25 us -> none  [the longest x2 17.2 us: route(): lax.all_to_all(packed_codes.reshape(owner_count, capacity), 'own', split_...]
    scatter x4 -> x0, local copies, waits for them, and re-layouts: 17.5 us -> none  [the longest x2 8.81 us: route(): source_row = jnp.zeros((slot_total,), jnp.int32).at[target].set(jnp.arang...]
  transfers between devices with their start and end apart: 6 -> 0, of which waited for: 5 -> 0; matrix products, arithmetic and copies ran while one was open for 7% -> 0% of each run, Pallas kernels for 0% -> 0%
where the time goes in v1:
time: 232 us
  Pallas kernels  223 us (96%)
  local copies, waits for them, and re-layouts  6.81 us (3%)
    pallas_call x1, Pallas kernels, per_device(): pl.pallas_call(main_kernel, out_shape=(jax.ShapeDtypeStruct((ROWS, D), BF...  203 us
    pallas_call x1, Pallas kernels, per_device(): pl.pallas_call(prep_kernel, out_shape=(jax.ShapeDtypeStruct((CHUNKS, GROU...  19.4 us
    unnamed x12, local copies, waits for them, and re-layouts  6.59 us

profile of v1, /device:TPU:1, one launch (start us, length us, event | category | flops | bytes accessed | tf_op | source)
XLA Modules:
  0.0 231.7 jit_solution(11467590273418193249)
XLA Ops:
  0.6 0.7 pad_add_fusion.lane_ref
  1.3 0.7 pad_add_fusion.1
  2.1 0.2 copy.7.col_ref
  2.3 0.0 copy-start
  2.3 1.2 copy-done
  3.5 19.4 %shard_map.50 = (bf16[2,16,128,256]{3,2,1,0:T(8,128)(2,1)}, s32[16,8,128]{2,1,0:T(8,128)S(1)}, s32[2,16,128,2]{3,2,1,0:T(8,128)}, s32[16,8,128]{2,1,0:T(8,128)S(1)}, s32[1024,1]{1,0:T(8,128)S(1)}) custom-call(s32[2,1024]{1,0:T(2,128)S(1)} %pad_add_fusion.lane_ref, s32[1024,2]{1,0:T(8,128)S(1)} %copy.7.col_ref, bf16[1024,512]{1,0:T(8,128)(2,1)S(1)} %copy-done), custom_call_target="tpu_custom_call" | custom-call | tf_op jit(solution)/shard_map/pallas_call | solution.py:385
  22.9 0.0 copy-start.1
  22.9 0.8 copy-done.1
  23.7 0.0 copy-start.2
  23.7 0.6 copy-done.2
  24.3 0.0 copy-start.3
  24.3 0.6 copy-done.3
  24.9 203.4 %shard_map.51 = (bf16[1024,512]{1,0:T(8,128)(2,1)}, bf16[1024,512]{1,0:T(8,128)(2,1)}) custom-call(bf16[2,16,128,256]{3,2,1,0:T(8,128)(2,1)} %get-tuple-element.7.packed1, s32[16,8,128]{2,1,0:T(8,128)} %copy-done.2, s32[2,16,128,2]{3,2,1,0:T(8,128)} %get-tuple-element.9.scol, s32[16,8,128]{2,1,0:T(8,128)} %copy-done.3, s32[1024,1]{1,0:T(8,128)} %copy-done.1), custom_call_target="tpu_custom_call" | custom-call | tf_op jit(solution)/shard_map/pallas_call | solution.py:400
  228.3 0.0 copy-start.4
  228.3 2.4 %copy.10 = bf16[1024,512]{1,0:T(8,128)(2,1)} copy(bf16[1024,512]{1,0:T(8,128)(2,1)} %get-tuple-element.14) | data formatting | bytes 2097152
  230.7 0.0 copy-done.4
  230.7 1.0 copy.11
Async XLA Ops:
  2.3 1.2 copy-start
  22.9 0.8 copy-start.1
  23.7 0.6 copy-start.2
  24.3 0.6 copy-start.3
  228.3 2.4 %copy-start.4 = (bf16[1024,512]{1,0:T(8,128)(2,1)S(1)}, bf16[1024,512]{1,0:T(8,128)(2,1)}, u32[]{:S(2)}) copy-start(bf16[1024,512]{1,0:T(8,128)(2,1)} %get-tuple-element.15) | copy-start | bytes 3145732

commit v2 on v1

v2 whole, which is shorter than its diff:
```python
import functools

import jax
import jax.numpy as jnp
from jax import lax
from jax.experimental import pallas as pl
from jax.experimental.pallas import tpu as pltpu
from jax.sharding import PartitionSpec as P

ROWS = 1024
D = 512
GROUPS = 16
CAP = 128
QUAD = 4 * CAP
SLOTS = GROUPS * CAP
GCODES = 512
ITEMS_PER_CODE = 32
CHUNKS = 2
W = D // CHUNKS
HALF = GCODES // 2
ZN = 8
ZC = HALF // ZN
LAG = 5.0
BF = jnp.bfloat16
F32 = jnp.float32
I32 = jnp.int32
NT = (((1,), (1,)), ((), ()))
NEAR_FIRST = (1, 7, 2, 6, 3, 5, 4)
QUADS = (0, 1, 3, 2)


def iota(shape, dim):
    return lax.broadcasted_iota(I32, shape, dim)


def hot(mask):
    return jnp.where(mask, 1.0, 0.0).astype(BF)


def slots_of(codes):
    groups = [lax.shift_right_logical(k, 9) for k in codes]
    ones = jnp.concatenate(
        [jnp.where(iota((GROUPS, ROWS), 0) == g, 1.0, 0.0) for g in groups], axis=0
    )
    blocks = ROWS // CAP
    stack = jnp.concatenate([ones[:, b * CAP : (b + 1) * CAP] for b in range(blocks)], axis=0)
    before = hot(iota((CAP, CAP), 0) < iota((CAP, CAP), 1))
    within = jnp.dot(stack.astype(BF), before, preferred_element_type=F32)
    total = jnp.sum(stack, axis=1, keepdims=True)
    n = 2 * GROUPS
    prefix = jnp.zeros((n, 1), F32)
    out = [[], []]
    for b in range(blocks):
        part = slice(b * n, (b + 1) * n)
        rank = (within[part] + prefix) * stack[part]
        prefix = prefix + total[part]
        for l in range(2):
            r = jnp.sum(rank[l * GROUPS : (l + 1) * GROUPS], axis=0, keepdims=True)
            out[l].append(groups[l][:, b * CAP : (b + 1) * CAP] * CAP + r.astype(I32))
    return [jnp.concatenate(o, axis=1) for o in out]


def main_kernel(
    rows_in, code_one, code_two,
    final_out, near_out,
    packed1, packed2, codes_out, codes_in, scol, tgt2,
    got, acc, half_out, half_in, zpart, zin, table, move, back, secp, nearacc, nearp,
    code_s, code_r, a2a_s, a2a_r, hs, hr, rzs, rzr, azs, azr, xs, xr, ss, sr,
):
    own = lax.axis_index("own")
    me = lax.axis_index("pair")
    z, c = lax.div(own, 2), lax.rem(own, 2)
    y, x = lax.div(me, 4), lax.rem(me, 4)
    sib = z * 2 + (1 - c)

    def at(dy, dx):
        return lax.rem(y + dy, 4) * 4 + lax.rem(x + dx, 4)

    def zat(dz):
        return lax.rem(z + dz, ZN) * 2 + c

    barrier = pltpu.get_barrier_semaphore()

    def greet(o, p):
        pl.semaphore_signal(barrier, inc=1, device_id=(o, p), device_id_type=pl.DeviceIdType.MESH)

    for d in range(1, 16):
        greet(own, at(d // 4, d % 4))
    for dz in range(1, ZN):
        greet(zat(dz), me)
    greet(sib, me)

    started = []

    def copy(src, dst, s, r, o, p):
        return pltpu.make_async_remote_copy(
            src_ref=src, dst_ref=dst, send_sem=s, recv_sem=r,
            device_id=(o, p), device_id_type=pl.DeviceIdType.MESH,
        )

    def send(src, dst, s, r, o, p):
        k = copy(src, dst, s, r, o, p)
        k.start()
        started.append(k)

    def arrive(dst, s, r):
        copy(dst, dst, s, r, own, at(0, 1)).wait_recv()

    packs = (packed1, packed2)

    codes = [
        jnp.concatenate([ref[b : b + 1, :] for b in range(8)], axis=1)
        for ref in (code_one, code_two)
    ]
    target = slots_of(codes)
    item = iota((1, ROWS), 1)

    def place_of(l, oy):
        return hot(iota((QUAD, ROWS), 0) + oy * QUAD == target[l])

    def note_slots(l, oy, place):
        local = jnp.bitwise_and(codes[l], GCODES - 1)
        feats = jnp.concatenate(
            [
                lax.shift_right_logical(local, 4),
                jnp.bitwise_and(local, 15),
                lax.shift_right_logical(item, 5),
                jnp.bitwise_and(item, 31),
                jnp.ones_like(item),
                jnp.zeros((3, ROWS), I32),
            ],
            axis=0,
        ).astype(F32).astype(BF)
        v = lax.dot_general(feats, place, NT, preferred_element_type=F32)
        dead = v[4:5] - 1.0
        vals = jnp.concatenate(
            [
                v[0:1] * 16.0 + v[1:2] + dead,
                v[2:3] * 32.0 + v[3:4] + dead * (1.0 + l),
                jnp.zeros((6, QUAD), F32),
            ],
            axis=0,
        )
        ints = vals.astype(I32)
        for j in range(4):
            codes_out[l, oy * 4 + j] = ints[:, j * CAP : (j + 1) * CAP]
        scol[l, pl.ds(pl.multiple_of(oy * QUAD, QUAD), QUAD), :] = jnp.transpose(vals).astype(I32)

    def send_codes(l, dy, dx):
        d, to = dy * 4 + dx, at(dy, dx)
        send(codes_out.at[l, to], codes_in.at[l, d], code_s.at[l, d], code_r.at[l, d], own, to)

    def send_rows(l, ch, dy, dx):
        d, to = dy * 4 + dx, at(dy, dx)
        send(packs[l].at[ch, to], got.at[l, ch, d], a2a_s.at[l, ch, d], a2a_r.at[l, ch, d], own, to)

    def sum_rows(l, ch, q):
        if q == 0:
            got[l, ch, 0] = packs[l][ch, me]
        for d in range(4 * q, 4 * q + 4):
            if d:
                arrive(got.at[l, ch, d], a2a_s.at[l, ch, d], a2a_r.at[l, ch, d])
                if ch == 0:
                    arrive(codes_in.at[l, d], code_s.at[l, d], code_r.at[l, d])
        ks = jnp.concatenate([codes_in[l, d, 0:1, :] for d in range(4 * q, 4 * q + 4)], axis=1)
        pick = hot(iota((GCODES, QUAD), 0) == ks)
        part = jnp.dot(pick, got[l, ch, 4 * q : 4 * q + 4].reshape(QUAD, W), preferred_element_type=F32)
        if q == QUADS[0]:
            acc[ch] = part
        else:
            acc[ch] += part

    def exchange(l, ch):
        half_out[l, ch] = acc[ch, pl.ds(pl.multiple_of((1 - c) * HALF, HALF), HALF)].astype(BF)
        send(half_out.at[l, ch], half_in.at[l, ch], hs.at[l, ch], hr.at[l, ch], sib, me)

    def reduce_z(l, ch):
        arrive(half_in.at[l, ch], hs.at[l, ch], hr.at[l, ch])
        mine = pl.ds(pl.multiple_of(c * HALF, HALF), HALF)
        both = acc[ch, mine] + half_in[l, ch].astype(F32)
        acc[ch, mine] = both
        zpart[l, ch] = both.astype(BF)
        for dz in NEAR_FIRST:
            to = lax.rem(z + dz, ZN)
            send(zpart.at[l, ch, pl.ds(pl.multiple_of(to * ZC, ZC), ZC)], zin.at[l, ch, dz],
                 rzs.at[l, ch, dz], rzr.at[l, ch, dz], zat(dz), me)

    def gather_z(l, ch):
        total = acc[ch, pl.ds(pl.multiple_of(c * HALF + z * ZC, ZC), ZC)]
        for dz in NEAR_FIRST:
            arrive(zin.at[l, ch, dz], rzs.at[l, ch, dz], rzr.at[l, ch, dz])
            total += zin[l, ch, dz].astype(F32)
        mine = pl.ds(pl.multiple_of(z * ZC, ZC), ZC)
        table[l, ch, 0, c, mine, :] = (total * (1.0 / ITEMS_PER_CODE)).astype(BF)
        for dz in NEAR_FIRST:
            here = table.at[l, ch, 0, c, mine]
            send(here, here, azs.at[l, ch, dz], azr.at[l, ch, dz], zat(dz), me)

    def turn(da, db):
        return da * (1 - c) + db * c, db * (1 - c) + da * c

    def slot(da, db):
        dy, dx = turn(da, db)
        return dy * 4 + dx

    def side(da, db):
        dy, dx = turn(da, db)
        return at(dy, dx)

    def to_sibling(l, ch, da, db):
        here = table.at[l, ch, slot(da, db), c]
        u = da * 4 + db
        send(here, here, ss.at[l, ch, u], sr.at[l, ch, u], sib, me)

    def piece(l, ch, da, db, part):
        if part is None:
            return table.at[l, ch, slot(da, db), c]
        return table.at[l, ch, slot(da, db), c, pl.ds(part * (HALF // 2), HALF // 2)]

    def pass_on(l, ch, source, dest, k, step, part):
        send(piece(l, ch, *source, part), piece(l, ch, *dest, part), xs.at[l, ch, k], xr.at[l, ch, k],
             own, side(*step))

    def come(l, ch, dest, k, part=None):
        arrive(piece(l, ch, *dest, part), xs.at[l, ch, k], xr.at[l, ch, k])

    def second_axis(l, ch, da):
        pass_on(l, ch, (da, 0), (da, 1), 4 + 4 * da, (0, 1), None)
        pass_on(l, ch, (da, 0), (da, 3), 5 + 4 * da, (0, 3), None)

    def start_plane(l, ch):
        here = table.at[l, ch, 0, c, pl.ds(0, ZC)]
        for dz in NEAR_FIRST:
            arrive(here, azs.at[l, ch, dz], azr.at[l, ch, dz])
        pass_on(l, ch, (0, 0), (1, 0), 0, (1, 0), None)
        pass_on(l, ch, (0, 0), (3, 0), 1, (3, 0), None)
        second_axis(l, ch, 0)
        to_sibling(l, ch, 0, 0)

    def first_hop(l, ch, da):
        k = 0 if da == 1 else 1
        come(l, ch, (da, 0), k)
        pass_on(l, ch, (da, 0), (2, 0), 2 + k, (da, 0), k)
        second_axis(l, ch, da)
        to_sibling(l, ch, da, 0)

    def first_far(l, ch):
        come(l, ch, (2, 0), 2, 0)
        come(l, ch, (2, 0), 3, 1)
        second_axis(l, ch, 2)
        to_sibling(l, ch, 2, 0)

    def second_hop(l, ch, da):
        for k, db in ((0, 1), (1, 3)):
            come(l, ch, (da, db), 4 + 4 * da + k)
            pass_on(l, ch, (da, db), (da, 2), 6 + 4 * da + k, (0, db), k)
            to_sibling(l, ch, da, db)

    def second_far(l, ch, da):
        come(l, ch, (da, 2), 6 + 4 * da, 0)
        come(l, ch, (da, 2), 7 + 4 * da, 1)
        to_sibling(l, ch, da, 2)

    def plane(l, ch, use):
        yield 3.0
        first_hop(l, ch, 1)
        first_hop(l, ch, 3)
        yield 0.5
        second_hop(l, ch, 0)
        use(0, 0)
        yield 2.0
        first_far(l, ch)
        yield 0.5
        second_hop(l, ch, 1)
        use(1, 0)
        use(0, 1)
        yield 0.5
        second_hop(l, ch, 3)
        use(3, 0)
        use(0, 3)
        yield 0.5
        second_far(l, ch, 0)
        yield 2.0
        second_hop(l, ch, 2)
        use(1, 1)
        use(1, 3)
        yield 1.0
        second_far(l, ch, 1)
        use(3, 1)
        use(3, 3)
        yield 0.5
        second_far(l, ch, 3)
        use(2, 0)
        use(0, 2)
        yield 2.0
        second_far(l, ch, 2)
        for da, db in ((1, 2), (2, 1), (3, 2), (2, 3), (2, 2)):
            use(da, db)

    def ready(l, ch, da, db):
        u = db * 4 + da
        dy, dx = turn(da, db)
        s = dy * 4 + dx
        arrive(table.at[l, ch, s, 1 - c], ss.at[l, ch, u], sr.at[l, ch, u])
        o = at(4 - dy, 4 - dx)
        place = pl.ds(pl.multiple_of(o * CAP, CAP), CAP)
        pick = hot(iota((CAP, GCODES), 1) == scol[l, place, 0:1])
        cents = table[l, ch, s].reshape(GCODES, W)
        return o, place, cents, jnp.dot(pick, cents, preferred_element_type=F32)

    def use_one(ch, da, db):
        o, place, _, picked = ready(0, ch, da, db)
        secp[ch, place, :] = (packed1[ch, o].astype(F32) - picked).astype(BF)

    def use_two(ch, da, db):
        o, place, cents, picked = ready(1, ch, da, db)
        rows = packed2[ch, o]
        wide = rows.astype(F32)
        secp[ch, place, :] = (wide - picked).astype(BF)
        prods = lax.dot_general(rows, cents, NT, preferred_element_type=F32)
        sq = jnp.sum(wide * wide, axis=1, keepdims=True)
        cw = cents.astype(F32)
        cw = cw * cw
        top = cw.astype(BF)
        low = (cw - top.astype(F32)).astype(BF)
        ones = jnp.ones((8, W), BF)
        csq = lax.dot_general(ones, top, NT, preferred_element_type=F32)
        csq += lax.dot_general(ones, low, NT, preferred_element_type=F32)
        part = sq - 2.0 * prods + csq[0:1]
        if ch == 0:
            nearacc[place, :] = part
        elif ch < CHUNKS - 1:
            nearacc[place, :] += part
        else:
            nearp[place, :] = ((nearacc[place, :] + part) * (1.0 / D)).astype(BF)

    quads_out = (1, 3, 0, 2)
    for ch in range(CHUNKS):
        for dy in quads_out:
            oy = lax.rem(y + dy, 4)
            place = place_of(0, oy)
            if ch == 0:
                note_slots(0, oy, place)
            got_rows = jnp.dot(place, rows_in[:, ch * W : (ch + 1) * W], preferred_element_type=F32)
            packed1[ch, pl.ds(oy * 4, 4)] = got_rows.astype(BF).reshape(4, CAP, W)
            if ch == 0 and dy == quads_out[0]:
                pl.semaphore_wait(barrier, 15 + ZN - 1 + 1)
            for dx in (1, 3, 0, 2):
                if dy or dx:
                    if ch == 0:
                        send_codes(0, dy, dx)
                    send_rows(0, ch, dy, dx)
    codes_in[0, 0] = codes_out[0, me]

    for dy in quads_out:
        oy = lax.rem(y + dy, 4)
        note_slots(1, oy, place_of(1, oy))
        for dx in (1, 3, 0, 2):
            if dy or dx:
                send_codes(1, dy, dx)
    codes_in[1, 0] = codes_out[1, me]
    tgt2[...] = jnp.transpose(jnp.broadcast_to(target[1].astype(F32), (8, ROWS))).astype(I32)
    first_items = jnp.concatenate([codes_out[0, o, 1:2, :] for o in range(GROUPS)], axis=1)

    def build_move(o, carry):
        rows = pl.ds(pl.multiple_of(o * CAP, CAP), CAP)
        move[rows, :] = hot(first_items == scol[1, rows, 1:2])
        return carry

    lax.fori_loop(0, GROUPS, build_move, 0)

    def build_back(b, carry):
        rows = pl.ds(pl.multiple_of(b * CAP, CAP), CAP)
        back[rows, :] = hot(iota((CAP, SLOTS), 1) == tgt2[rows, 0:1])
        return carry

    lax.fori_loop(0, ROWS // CAP, build_back, 0)

    def chain(ch):
        for l in range(2):
            for q in QUADS:
                sum_rows(l, ch, q)
                yield 1.0
            exchange(l, ch)
            yield 2.0
            reduce_z(l, ch)
            yield 4.0
            gather_z(l, ch)
            yield 4.0
            start_plane(l, ch)
            if l == 0:
                yield from plane(0, ch, functools.partial(use_one, ch))
                for dy in quads_out:
                    oy = lax.rem(y + dy, 4)
                    rows = move[pl.ds(pl.multiple_of(oy * QUAD, QUAD), QUAD), :]
                    moved = jnp.dot(rows, secp[ch], preferred_element_type=F32).astype(BF)
                    packed2[ch, pl.ds(oy * 4, 4)] = moved.reshape(4, CAP, W)
                    for dx in (1, 3, 0, 2):
                        if dy or dx:
                            send_rows(1, ch, dy, dx)
                    yield 0.5
                yield 10.0
            else:
                yield from plane(1, ch, functools.partial(use_two, ch))
                for b in range(2):
                    rows = back[b * 512 : (b + 1) * 512, :]
                    out = jnp.dot(rows, secp[ch], preferred_element_type=F32).astype(BF)
                    final_out[b * 512 : (b + 1) * 512, ch * W : (ch + 1) * W] = out
                    yield 0.5

    chains = [[ch * LAG, ch, chain(ch)] for ch in range(CHUNKS)]
    while chains:
        first = min(chains, key=lambda k: (k[0], k[1]))
        pause = next(first[2], None)
        if pause is None:
            chains.remove(first)
        else:
            first[0] += pause

    for b in range(2):
        rows = back[b * 512 : (b + 1) * 512, :]
        near_out[b * 512 : (b + 1) * 512, :] = jnp.dot(rows, nearp[...], preferred_element_type=F32).astype(BF)
    for k in started:
        k.wait_send()


def per_device(residual, code_one, code_two):
    dma = pltpu.SemaphoreType.DMA
    C = CHUNKS
    vmem = pl.BlockSpec(memory_space=pltpu.VMEM)
    return pl.pallas_call(
        main_kernel,
        out_shape=(
            jax.ShapeDtypeStruct((ROWS, D), BF),
            jax.ShapeDtypeStruct((ROWS, D), BF),
        ),
        in_specs=[vmem] * 3,
        out_specs=(vmem, vmem),
        scratch_shapes=[
            pltpu.VMEM((C, GROUPS, CAP, W), BF),
            pltpu.VMEM((C, GROUPS, CAP, W), BF),
            pltpu.VMEM((2, GROUPS, 8, CAP), I32),
            pltpu.VMEM((2, GROUPS, 8, CAP), I32),
            pltpu.VMEM((2, SLOTS, 8), I32),
            pltpu.VMEM((ROWS, 8), I32),
            pltpu.VMEM((2, C, GROUPS, CAP, W), BF),
            pltpu.VMEM((C, GCODES, W), F32),
            pltpu.VMEM((2, C, HALF, W), BF),
            pltpu.VMEM((2, C, HALF, W), BF),
            pltpu.VMEM((2, C, HALF, W), BF),
            pltpu.VMEM((2, C, ZN, ZC, W), BF),
            pltpu.VMEM((2, C, GROUPS, 2, HALF, W), BF),
            pltpu.VMEM((SLOTS, SLOTS), BF),
            pltpu.VMEM((ROWS, SLOTS), BF),
            pltpu.VMEM((C, SLOTS, W), BF),
            pltpu.VMEM((SLOTS, D), F32),
            pltpu.VMEM((SLOTS, D), BF),
            dma((2, GROUPS)), dma((2, GROUPS)),
            dma((2, C, GROUPS)), dma((2, C, GROUPS)),
            dma((2, C)), dma((2, C)),
            dma((2, C, ZN)), dma((2, C, ZN)),
            dma((2, C, ZN)), dma((2, C, ZN)),
            dma((2, C, 20)), dma((2, C, 20)),
            dma((2, C, GROUPS)), dma((2, C, GROUPS)),
        ],
        compiler_params=pltpu.CompilerParams(
            collective_id=0, has_side_effects=True, vmem_limit_bytes=60 * 1024 * 1024
        ),
    )(residual, code_one.reshape(8, CAP), code_two.reshape(8, CAP))


def solution(mesh):
    in_specs = (P(("own", "pair"), None), P(("own", "pair")), P(("own", "pair")))
    out_specs = (P(("own", "pair"), None), P(("own", "pair"), None))
    return jax.shard_map(
        per_device, mesh=mesh, in_specs=in_specs, out_specs=out_specs, check_vma=False
    )
```

time: 232 us -> 160 us (0.69)
  Pallas kernels: 223 us -> 156 us
  local copies, waits for them, and re-layouts: 6.81 us -> 3.32 us
    pallas_call x1, Pallas kernels: 203 us -> 156 us  [per_device(): pl.pallas_call(main_kernel, out_shape=(jax.ShapeDtypeStruct((ROWS, D), BF...]
    pallas_call x1 -> x0, Pallas kernels: 19.4 us -> none  [per_device(): pl.pallas_call(prep_kernel, out_shape=(jax.ShapeDtypeStruct((CHUNKS, GROU...]
    unnamed x12 -> x4, local copies, waits for them, and re-layouts: 6.59 us -> 3.32 us
where the time goes in v2:
time: 160 us
  Pallas kernels  156 us (98%)
  local copies, waits for them, and re-layouts  3.32 us (2%)
    pallas_call x1, Pallas kernels, per_device(): pl.pallas_call(main_kernel, out_shape=(jax.ShapeDtypeStruct((ROWS, D), BF...  156 us
    unnamed x4, local copies, waits for them, and re-layouts  3.32 us

profile of v2, /device:TPU:1, one launch (start us, length us, event | category | flops | bytes accessed | tf_op | source)
XLA Modules:
  0.0 159.9 jit_solution(13955015981463637018)
XLA Ops:
  0.6 156.0 %shard_map.50 = (bf16[1024,512]{1,0:T(8,128)(2,1)}, bf16[1024,512]{1,0:T(8,128)(2,1)}) custom-call(bf16[1024,512]{1,0:T(8,128)(2,1)} %rows_in.1, s32[8,128]{1,0:T(8,128)} %bitcast.2, s32[8,128]{1,0:T(8,128)} %bitcast.3), custom_call_target="tpu_custom_call" | custom-call | tf_op jit(solution)/shard_map/pallas_call | solution.py:431
  156.6 0.0 copy-start
  156.6 2.4 %copy.7 = bf16[1024,512]{1,0:T(8,128)(2,1)} copy(bf16[1024,512]{1,0:T(8,128)(2,1)} %get-tuple-element.4) | data formatting | bytes 2097152
  159.0 0.0 copy-done
  159.0 1.0 copy.8
Async XLA Ops:
  156.6 2.4 %copy-start = (bf16[1024,512]{1,0:T(8,128)(2,1)S(1)}, bf16[1024,512]{1,0:T(8,128)(2,1)}, u32[]{:S(2)}) copy-start(bf16[1024,512]{1,0:T(8,128)(2,1)} %get-tuple-element.5) | copy-start | bytes 3145732
